TPU v7x, 128 devices: a whole 4x4x4 slice. The times are simulated.
128 devices in a mesh: head: 8 (over x, z_lo), tok: 16 (over z_hi, y, core).
Axes of the slice: x: 4, y: 4, z: 4 (z_hi: 2, z_lo: 2; z = z_hi * 2 + z_lo), core: 2. Of those that a mesh axis runs over, the one named last changes fastest.
Arguments:
- queries: bfloat16 [8192, 8192], P(('head', 'tok')), may hold values from -6 to 6
- keys: bfloat16 [8192, 8192], P(('head', 'tok')), may hold values from -6 to 6
- values: bfloat16 [8192, 8192], P(('head', 'tok')), may hold values from -6 to 6
- rates: bfloat16 [8192, 16], P(('head', 'tok')), may hold values from 0.049804688 to 1
- w_first: float32 [16, 512, 512], P('head'), may hold values from -0.25 to 0.25
- w_gate: float32 [16, 512, 512], P('head'), may hold values from -0.25 to 0.25
- w_second: float32 [16, 512, 512], P('head'), may hold values from -0.25 to 0.25
Outputs:
- mixed: bfloat16 [8192, 8192], P(('head', 'tok'))
- new_first: float32 [16, 512, 512], P('head')
- new_gate: float32 [16, 512, 512], P('head')
- new_second: float32 [16, 512, 512], P('head')
All inputs are finite; a program needn't handle non-finite values.
Results may differ from a plain program's by a relative error of at most 0.0072.
Values may be sent and summed in bfloat16 or wider, within the bound.
A program may use at most 128 MiB of HBM per device.

v0:
```python
import functools

import jax
import jax.numpy as jnp
from jax import lax
from jax.experimental import pallas as pl
from jax.experimental.pallas import tpu as pltpu
from jax.sharding import PartitionSpec as P

ITERS = 3
BF = jnp.bfloat16
F32 = jnp.float32
MESH = pl.DeviceIdType.MESH
GROUPS = 8
ROWS = 64
DH = 512
HALF = 256
SPAN = GROUPS * ROWS
TILE = 256
NT = (((1,), (1,)), ((), ()))
TN = (((0,), (0,)), ((), ()))
OFFSETS = ((1, 0), (3, 0), (0, 1), (2, 1), (2, 0), (1, 1), (3, 1))


def kernel(
    q_hbm, k_hbm, v_hbm, r_hbm, w1_hbm, w3_hbm, w2_hbm,
    mixed, out1, out3, out2,
    wv, vv, rv, dv, kin, din, qin, wb13, wb2, oldn, dz, hid,
    gs13, gs2, ry13, ry2, py13, py2, zs13, zs2, rz13, rz2, gg13, gg2,
    xs, xb, nb, qh, ov,
    load_sem, a2a_s, a2a_r, fw_s, fw_r, ry_s, ry_r, rz_s, rz_r,
    az_s, az_r, ay_s, ay_r, fg_s, fg_r, o_s, o_r,
):
    hi = lax.axis_index("head")
    tk = lax.axis_index("tok")
    x, zl = hi // 2, lax.rem(hi, 2)
    zh, y, c = tk // 8, lax.rem(tk // 2, 4), lax.rem(tk, 2)
    peers = [lax.rem(x + dx, 4) * 2 + lax.rem(zl + dz_, 2) for dx, dz_ in OFFSETS]
    ypeers = [zh * 8 + lax.rem(y + o, 4) * 2 + c for o in (1, 2, 3)]
    zpeer = (1 - zh) * 8 + y * 2 + c
    sib = zh * 8 + y * 2 + (1 - c)

    def remote(src, dst, s, r, **where):
        return pltpu.make_async_remote_copy(
            src_ref=src, dst_ref=dst, send_sem=s, recv_sem=r, device_id=where, device_id_type=MESH
        )

    def done(ref, sem):
        pltpu.make_async_copy(ref, ref, sem).wait()

    loads = [pltpu.make_async_copy(v_hbm, vv, load_sem.at[0]), pltpu.make_async_copy(r_hbm, rv, load_sem.at[1])]
    loads += [
        pltpu.make_async_copy(w, wv.at[m], load_sem.at[2 + m]) for m, w in enumerate((w1_hbm, w3_hbm, w2_hbm))
    ]
    for copy in loads:
        copy.start()

    barrier = pltpu.get_barrier_semaphore()
    for p in peers:
        pl.semaphore_signal(barrier, inc=1, device_id={"head": p}, device_id_type=MESH)
    for p in ypeers + [zpeer, sib]:
        pl.semaphore_signal(barrier, inc=1, device_id={"tok": p}, device_id_type=MESH)
    pl.semaphore_wait(barrier, len(peers) + 5)

    slot = pl.ds(pl.multiple_of(hi * ROWS, ROWS), ROWS)

    def columns(p, h):
        return pl.ds(pl.multiple_of((2 * p + h) * DH, DH), DH)

    def scatter(src, land, i, h):
        for p in peers:
            remote(src.at[:, columns(p, h)], land.at[slot], a2a_s.at[i], a2a_r.at[i], head=p).start()
        pltpu.make_async_copy(src.at[:, columns(hi, h)], land.at[slot], a2a_r.at[i]).start()

    def rate_values(h):
        rates = rv[...].astype(F32)
        for g in range(h, 2 * GROUPS, 2):
            cols = slice(g * DH, (g + 1) * DH)
            dv[:, cols] = (-(rates[:, g : g + 1] * vv[:, cols].astype(F32))).astype(BF)

    scatter(k_hbm, kin.at[0, c], 0, 0)
    loads[0].wait()
    loads[1].wait()
    rate_values(0)
    scatter(dv, din.at[0, c], 1, 0)
    scatter(k_hbm, kin.at[1, c], 2, 1)
    rate_values(1)
    scatter(dv, din.at[1, c], 3, 1)

    for copy in loads[2:]:
        copy.wait()
    half = pl.ds(pl.multiple_of(c * HALF, HALF), HALF)
    for h in range(2):
        wb13[h, :, :HALF] = wv[0, h, :, half].astype(BF)
        wb13[h, :, HALF:] = wv[1, h, :, half].astype(BF)
        wb2[h] = wv[2, h, half, :].astype(BF)
        for m in range(3):
            w = wv[m, h]
            oldn[3 * h + m] = jnp.broadcast_to(
                jnp.sqrt(jnp.sum(w * w, axis=0, keepdims=True) + 1e-06), (8, DH)
            )

    def forward(h):
        for i, buf in enumerate((kin, din)):
            done(buf.at[h, c], a2a_r.at[2 * h + i])
            remote(buf.at[h, c], buf.at[h, c], fw_s.at[2 * h + i], fw_r.at[2 * h + i], tok=sib).start()

    def hidden_grads(h, core):
        @pl.loop(0, SPAN // TILE)
        def _(step):
            at = pl.ds(pl.multiple_of(step * TILE, TILE), TILE)
            z = jnp.dot(kin[h, core, at, :], wb13[h], preferred_element_type=F32)
            dh = lax.dot_general(din[h, core, at, :], wb2[h], NT, preferred_element_type=F32)
            z1, z3 = z[:, :HALF], z[:, HALF:]
            sg = 1.0 / (1.0 + jnp.exp(-z1))
            act = z1 * sg
            hid[core, at, :] = (act * z3).astype(BF)
            dz[core, at, :HALF] = (dh * z3 * sg * (1.0 + z1 * (1.0 - sg))).astype(BF)
            dz[core, at, HALF:] = (dh * act).astype(BF)

    def send_y(src, land, rows, sems, i):
        for o, p in zip((1, 2, 3), ypeers):
            block = pl.ds(pl.multiple_of(lax.rem(y + o, 4) * rows, rows), rows)
            remote(src.at[block], land.at[pl.ds((3 - o) * rows, rows)], ry_s.at[i], ry_r.at[i], tok=p).start()

    def weight_grads(h):
        @pl.loop(0, 4)
        def _(j):
            cols = pl.ds(pl.multiple_of(j * 128, 128), 128)
            g = lax.dot_general(kin[h, 0, :, cols], dz[0], TN, preferred_element_type=F32)
            g += lax.dot_general(kin[h, 1, :, cols], dz[1], TN, preferred_element_type=F32)
            gs13[h, cols, :] = g.astype(BF)

        send_y(gs13.at[h], ry13.at[h], 128, ry_s, 2 * h)

        @pl.loop(0, 2)
        def _(j):
            cols = pl.ds(pl.multiple_of(j * 128, 128), 128)
            g = lax.dot_general(hid[0, :, cols], din[h, 0], TN, preferred_element_type=F32)
            g += lax.dot_general(hid[1, :, cols], din[h, 1], TN, preferred_element_type=F32)
            gs2[h, cols, :] = g.astype(BF)

        send_y(gs2.at[h], ry2.at[h], 64, ry_s, 2 * h + 1)

    mats = ((gs13, ry13, py13, zs13, rz13, gg13, 128), (gs2, ry2, py2, zs2, rz2, gg2, 64))

    def reduce_y(h):
        for i, (gs, ry, py, zs, rz, gg, n) in enumerate(mats):
            done(ry.at[h], ry_r.at[2 * h + i])
            own = pl.ds(pl.multiple_of(y * n, n), n)
            total = gs[h, own, :].astype(F32)
            for o in range(3):
                total += ry[h, pl.ds(o * n, n), :].astype(F32)
            py[h] = total
            zs[h] = py[h, pl.ds(pl.multiple_of((1 - zh) * (n // 2), n // 2), n // 2), :].astype(BF)
            remote(zs.at[h], rz.at[h], rz_s.at[2 * h + i], rz_r.at[2 * h + i], tok=zpeer).start()

    def gather(h):
        for i, (gs, ry, py, zs, rz, gg, n) in enumerate(mats):
            k = n // 2
            done(rz.at[h], rz_r.at[2 * h + i])
            total = py[h, pl.ds(pl.multiple_of(zh * k, k), k), :] + rz[h].astype(F32)
            own = pl.ds(pl.multiple_of(y * n + zh * k, k), k)
            gg[h, c, own, :] = total.astype(BF)
            view = gg.at[h, c, own]
            remote(view, view, az_s.at[2 * h + i], az_r.at[2 * h + i], tok=zpeer).start()
            for p in ypeers:
                remote(view, view, ay_s.at[2 * h + i], ay_r.at[2 * h + i], tok=p).start()
        for i, (gs, ry, py, zs, rz, gg, n) in enumerate(mats):
            k = n // 2
            other = pl.ds(pl.multiple_of(y * n + (1 - zh) * k, k), k)
            view = gg.at[h, c, other]
            done(view, az_r.at[2 * h + i])
            for p in ypeers:
                remote(view, view, ay_s.at[2 * h + i], ay_r.at[2 * h + i], tok=p).start()

    def share(h):
        for i, (gs, ry, py, zs, rz, gg, n) in enumerate(mats):
            done(gg.at[h, c, pl.ds(0, 3 * n)], ay_r.at[2 * h + i])
            remote(gg.at[h, c], gg.at[h, c], fg_s.at[2 * h + i], fg_r.at[2 * h + i], tok=sib).start()

    outs = (out1, out3, out2)

    def newton(h, m):
        def g_part(part):
            if m == 2:
                return gg2[h, part].astype(F32)
            return gg13[h, part, :, m * HALF : (m + 1) * HALF].astype(F32)

        squares = jnp.sum(g_part(0) ** 2) + jnp.sum(g_part(1) ** 2)
        scale = 1.0 / (jnp.sqrt(jnp.full((8, 128), squares, F32)) + 1e-06)
        scale = scale[:1, :1]
        for part in range(2):
            piece = g_part(part) * scale
            where = pl.ds(part * HALF, HALF)
            if m == 2:
                xs[where, :] = piece
                xb[0, where, :] = piece.astype(BF)
            else:
                xs[:, where] = piece
                xb[0, :, where] = piece.astype(BF)
        for step in range(ITERS):
            now, later = step % 2, (step + 1) % 2

            @pl.loop(0, DH // TILE)
            def _(j):
                at = pl.ds(pl.multiple_of(j * TILE, TILE), TILE)
                square = lax.dot_general(xb[now, at, :], xb[now], NT, preferred_element_type=F32)
                cube = jnp.dot(square.astype(BF), xb[now], preferred_element_type=F32)
                fresh = 1.5 * xs[at, :] - 0.5 * cube
                xs[at, :] = fresh
                if step < ITERS - 1:
                    xb[later, at, :] = fresh.astype(BF)

        update = wv[m, h] - xs[...]
        new_norm = jnp.sqrt(jnp.sum(update * update, axis=0, keepdims=True) + 1e-06)
        fresh = update * (oldn[3 * h + m, :1, :] / new_norm)
        outs[m][h] = fresh
        nb[m] = fresh.astype(BF)

    def apply(h):
        done(qin.at[h], a2a_r.at[4 + h])

        @pl.loop(0, SPAN // TILE)
        def _(step):
            at = pl.ds(pl.multiple_of(step * TILE, TILE), TILE)
            q = qin[h, at, :]
            y1 = jnp.dot(q, nb[0], preferred_element_type=F32)
            y3 = jnp.dot(q, nb[1], preferred_element_type=F32)
            qh[...] = (y1 * (1.0 / (1.0 + jnp.exp(-y1))) * y3).astype(BF)
            ov[h, at, :] = jnp.dot(qh[...], nb[2], preferred_element_type=F32).astype(BF)

        for p in peers:
            rows = pl.ds(pl.multiple_of(p * ROWS, ROWS), ROWS)
            remote(ov.at[h, rows], mixed.at[:, columns(hi, h)], o_s.at[h], o_r.at[h], head=p).start()
        pltpu.make_async_copy(ov.at[h, slot], mixed.at[:, columns(hi, h)], o_r.at[h]).start()

    forward(0)
    hidden_grads(0, c)
    for i, buf in enumerate((kin, din)):
        done(buf.at[0, 1 - c], fw_r.at[i])
    hidden_grads(0, 1 - c)
    weight_grads(0)

    forward(1)
    scatter(q_hbm, qin.at[0], 4, 0)
    scatter(q_hbm, qin.at[1], 5, 1)
    hidden_grads(1, c)
    reduce_y(0)
    for i, buf in enumerate((kin, din)):
        done(buf.at[1, 1 - c], fw_r.at[2 + i])
    hidden_grads(1, 1 - c)
    weight_grads(1)
    gather(0)
    reduce_y(1)
    share(0)
    gather(1)
    for i, gg in enumerate((gg13, gg2)):
        done(gg.at[0, 1 - c], fg_r.at[i])
    for m in range(3):
        newton(0, m)
    share(1)
    apply(0)
    for i, gg in enumerate((gg13, gg2)):
        done(gg.at[1, 1 - c], fg_r.at[2 + i])
    for m in range(3):
        newton(1, m)
    apply(1)

    sent = kin.at[0, 0, pl.ds(0, SPAN - ROWS)]
    for h in range(2):
        done(kin.at[0, 0], o_r.at[h])
        done(sent, o_s.at[h])
    for i in range(6):
        done(sent, a2a_s.at[i])
    for h in range(2):
        for i, (gs, ry, py, zs, rz, gg, n) in enumerate(mats):
            j = 2 * h + i
            done(kin.at[0, 0], fw_s.at[j])
            done(gs.at[h, pl.ds(0, 3 * n)], ry_s.at[j])
            done(zs.at[h], rz_s.at[j])
            done(zs.at[h], az_s.at[j])
            done(gg.at[h, c, pl.ds(0, 3 * n)], ay_s.at[j])
            done(gg.at[h, c], fg_s.at[j])


def on_device(queries, keys, values, rates, w_first, w_gate, w_second):
    any_spec = pl.BlockSpec(memory_space=pl.ANY)
    vmem_spec = pl.BlockSpec(memory_space=pltpu.VMEM)
    dma = pltpu.SemaphoreType.DMA
    weights = jax.ShapeDtypeStruct(w_first.shape, F32)
    vm = pltpu.VMEM
    return pl.pallas_call(
        kernel,
        out_shape=(jax.ShapeDtypeStruct(queries.shape, BF), weights, weights, weights),
        in_specs=[any_spec] * 7,
        out_specs=(any_spec, vmem_spec, vmem_spec, vmem_spec),
        scratch_shapes=[
            vm((3, 2, DH, DH), F32),
            vm(values.shape, BF),
            vm(rates.shape, BF),
            vm(values.shape, BF),
            vm((2, 2, SPAN, DH), BF),
            vm((2, 2, SPAN, DH), BF),
            vm((2, SPAN, DH), BF),
            vm((2, DH, DH), BF),
            vm((2, HALF, DH), BF),
            vm((6, 8, DH), F32),
            vm((2, SPAN, DH), BF),
            vm((2, SPAN, HALF), BF),
            vm((2, DH, DH), BF),
            vm((2, HALF, DH), BF),
            vm((2, 384, DH), BF),
            vm((2, 192, DH), BF),
            vm((2, 128, DH), F32),
            vm((2, 64, DH), F32),
            vm((2, 64, DH), BF),
            vm((2, 32, DH), BF),
            vm((2, 64, DH), BF),
            vm((2, 32, DH), BF),
            vm((2, 2, DH, DH), BF),
            vm((2, 2, HALF, DH), BF),
            vm((DH, DH), F32),
            vm((2, DH, DH), BF),
            vm((3, DH, DH), BF),
            vm((TILE, DH), BF),
            vm((2, SPAN, DH), BF),
            dma((5,)), dma((6,)), dma((6,)), dma((4,)), dma((4,)), dma((4,)), dma((4,)),
            dma((4,)), dma((4,)), dma((4,)), dma((4,)), dma((4,)), dma((4,)), dma((4,)),
            dma((4,)), dma((2,)), dma((2,)),
        ],
        compiler_params=pltpu.CompilerParams(
            collective_id=0, has_side_effects=True, vmem_limit_bytes=56 * 1024 * 1024
        ),
        name="layer",
    )(queries, keys, values, rates, w_first, w_gate, w_second)


def solution(mesh):
    placed = (
        P(("head", "tok"), None),
        P(("head", "tok"), None),
        P(("head", "tok"), None),
        P(("head", "tok"), None),
        P("head", None, None),
        P("head", None, None),
        P("head", None, None),
    )
    return jax.shard_map(
        on_device,
        mesh=mesh,
        in_specs=placed,
        out_specs=(
            P(("head", "tok"), None),
            P("head", None, None),
            P("head", None, None),
            P("head", None, None),
        ),
        check_vma=False,
    )
```

profile of v0, /device:TPU:1, one launch (start us, length us, event | category | flops | bytes accessed | tf_op | source)
XLA Modules:
  0.0 113.8 jit_solution(2911801768004605634)
XLA Ops:
  0.6 1.4 %copy.11.r_hbm = bf16[64,16]{1,0:T(8,128)(2,1)} copy(bf16[64,16]{0,1:T(8,128)(2,1)} %param.10) | data formatting | bytes 4096 | tf_op args[3]
  2.0 103.4 %layer.1 = (bf16[64,8192]{1,0:T(8,128)(2,1)}, f32[2,512,512]{2,1,0:T(8,128)}, f32[2,512,512]{2,1,0:T(8,128)}, f32[2,512,512]{2,1,0:T(8,128)}) custom-call(bf16[64,8192]{1,0:T(8,128)(2,1)} %q_hbm.1, bf16[64,8192]{1,0:T(8,128)(2,1)} %k_hbm.1, bf16[64,8192]{1,0:T(8,128)(2,1)} %v_hbm.1, bf16[64,16]{1,0:T(8,128)(2,1)} %copy.11.r_hbm, f32[2,512,512]{2,1,0:T(8,128)} %w1_hbm.1, ...), custom_call_target="tpu_custom_call" | custom-call | tf_op jit(solution)/shard_map/layer/pallas_call | solution.py:293
  105.4 0.0 copy-start.2
  105.4 2.4 %copy.16 = bf16[64,8192]{1,0:T(8,128)(2,1)} copy(bf16[64,8192]{1,0:T(8,128)(2,1)} %get-tuple-element.8) | data formatting | bytes 2097152
  107.8 0.0 copy-done.2
  107.8 0.0 copy-start.1
  107.8 1.3 %copy.17 = f32[2,512,512]{2,1,0:T(8,128)} copy(f32[2,512,512]{2,1,0:T(8,128)S(1)} %copy-done.2) | data formatting | bytes 4194304
  109.1 1.0 copy-done.1
  110.2 0.0 copy-start
  110.2 1.3 %copy.18 = f32[2,512,512]{2,1,0:T(8,128)} copy(f32[2,512,512]{2,1,0:T(8,128)S(1)} %copy-done.1) | data formatting | bytes 4194304
  111.5 1.0 copy-done
  112.5 1.3 %copy.19 = f32[2,512,512]{2,1,0:T(8,128)} copy(f32[2,512,512]{2,1,0:T(8,128)S(1)} %copy-done) | data formatting | bytes 4194304
Async XLA Ops:
  105.4 2.4 %copy-start.2 = (f32[2,512,512]{2,1,0:T(8,128)S(1)}, f32[2,512,512]{2,1,0:T(8,128)}, u32[]{:S(2)}) copy-start(f32[2,512,512]{2,1,0:T(8,128)} %get-tuple-element.9) | copy-start | bytes 6291460
  107.8 2.3 %copy-start.1 = (f32[2,512,512]{2,1,0:T(8,128)S(1)}, f32[2,512,512]{2,1,0:T(8,128)}, u32[]{:S(2)}) copy-start(f32[2,512,512]{2,1,0:T(8,128)} %get-tuple-element.10) | copy-start | bytes 6291460
  110.2 2.3 %copy-start = (f32[2,512,512]{2,1,0:T(8,128)S(1)}, f32[2,512,512]{2,1,0:T(8,128)}, u32[]{:S(2)}) copy-start(f32[2,512,512]{2,1,0:T(8,128)} %get-tuple-element.11) | copy-start | bytes 6291460
where the time goes:
time: 114 us
  Pallas kernels  103 us (90%)
  local copies, waits for them, and re-layouts  9.8 us (9%)
    pallas_call x1, Pallas kernels, on_device(): pl.pallas_call(kernel, out_shape=(jax.ShapeDtypeStruct(queries.shape, BF)...  103 us
    unnamed x11, local copies, waits for them, and re-layouts  9.8 us

commit v1 on v0

v1 whole, which is shorter than its diff:
```python
import functools

import jax
import jax.numpy as jnp
from jax import lax
from jax.experimental import pallas as pl
from jax.experimental.pallas import tpu as pltpu
from jax.sharding import PartitionSpec as P

ITERS = 3
BF = jnp.bfloat16
F32 = jnp.float32
MESH = pl.DeviceIdType.MESH
GROUPS = 8
ROWS = 64
DH = 512
HALF = 256
VMEM_BYTES = 56 * 1024 * 1024
SPAN = GROUPS * ROWS
TILE = 256
NT = (((1,), (1,)), ((), ()))
TN = (((0,), (0,)), ((), ()))
OFFSETS = ((2, 1), (2, 0), (1, 1), (3, 1), (1, 0), (3, 0), (0, 1))
BACK = tuple(OFFSETS.index(((4 - dx) % 4, dz)) for dx, dz in OFFSETS)
OWN = len(OFFSETS)


def kernel(
    q_hbm, k_hbm, v_hbm, r_hbm, w1_hbm, w3_hbm, w2_hbm,
    mixed, out1, out3, out2,
    wv, vv, rv, dv, kin, din, qin, wb13, wb2, oldn, dz, hid,
    gs13, gs2, ry13, ry2, py13, py2, zs13, zs2, rz13, rz2, gg13, gg2,
    xs, xb, nb, qh, ov, nf,
    load_sem, a2a_s, a2a_r, fw_s, fw_r, ry_s, ry_r, rz_s, rz_r,
    az_s, az_r, ay_s, ay_r, fg_s, fg_r, o_s, o_r, nf_sem,
):
    hi = lax.axis_index("head")
    tk = lax.axis_index("tok")
    x, zl = hi // 2, lax.rem(hi, 2)
    zh, y, c = tk // 8, lax.rem(tk // 2, 4), lax.rem(tk, 2)
    peers = [lax.rem(x + dx, 4) * 2 + lax.rem(zl + dz_, 2) for dx, dz_ in OFFSETS]
    ypeers = [zh * 8 + lax.rem(y + o, 4) * 2 + c for o in (1, 2, 3)]
    zpeer = (1 - zh) * 8 + y * 2 + c
    sib = zh * 8 + y * 2 + (1 - c)

    def remote(src, dst, s, r, **where):
        return pltpu.make_async_remote_copy(
            src_ref=src, dst_ref=dst, send_sem=s, recv_sem=r, device_id=where, device_id_type=MESH
        )

    pending = {}

    def done(name, i):
        ref, sem = pending.pop((name, i))
        pltpu.make_async_copy(ref, ref, sem).wait()

    def track(name, i, sent, arriving, send_sems, recv_sems):
        pending[name + "_s", i] = (sent, send_sems.at[i])
        pending[name, i] = (arriving, recv_sems.at[i])

    loads = [pltpu.make_async_copy(v_hbm, vv, load_sem.at[0]), pltpu.make_async_copy(r_hbm, rv, load_sem.at[1])]
    loads += [
        pltpu.make_async_copy(w, wv.at[m], load_sem.at[2 + m]) for m, w in enumerate((w1_hbm, w3_hbm, w2_hbm))
    ]
    for copy in loads:
        copy.start()

    barrier = pltpu.get_barrier_semaphore()
    for p in peers:
        pl.semaphore_signal(barrier, inc=1, device_id={"head": p}, device_id_type=MESH)
    for p in ypeers + [zpeer, sib]:
        pl.semaphore_signal(barrier, inc=1, device_id={"tok": p}, device_id_type=MESH)
    pl.semaphore_wait(barrier, len(peers) + 5)

    def slot(i):
        return pl.ds(i * ROWS, ROWS)

    def columns(p, h):
        return pl.ds(pl.multiple_of((2 * p + h) * DH, DH), DH)

    def scatter(src, land, i, h):
        for p, b in zip(peers, BACK):
            remote(src.at[:, columns(p, h)], land.at[slot(b)], a2a_s.at[i], a2a_r.at[i], head=p).start()
        pltpu.make_async_copy(src.at[:, columns(hi, h)], land.at[slot(OWN)], a2a_r.at[i]).start()
        track("a2a", i, land.at[pl.ds(0, SPAN - ROWS)], land, a2a_s, a2a_r)

    def rate_values(h):
        rates = rv[...].astype(F32).T
        for g in range(h, 2 * GROUPS, 2):
            cols = slice(g * DH, (g + 1) * DH)
            dv[:, cols] = (-(rates[:, g : g + 1] * vv[:, cols].astype(F32))).astype(BF)

    scatter(k_hbm, kin.at[0, c], 0, 0)
    loads[0].wait()
    loads[1].wait()
    rate_values(0)
    scatter(dv, din.at[0, c], 1, 0)
    scatter(k_hbm, kin.at[1, c], 2, 1)
    rate_values(1)
    scatter(dv, din.at[1, c], 3, 1)

    for copy in loads[2:]:
        copy.wait()
    half = pl.ds(pl.multiple_of(c * HALF, HALF), HALF)
    for h in range(2):
        wb13[h, :, :HALF] = wv[0, h, :, half].astype(BF)
        wb13[h, :, HALF:] = wv[1, h, :, half].astype(BF)
        wb2[h] = wv[2, h, half, :].astype(BF)
        for m in range(3):
            w = wv[m, h]
            oldn[3 * h + m] = jnp.broadcast_to(
                jnp.sqrt(jnp.sum(w * w, axis=0, keepdims=True) + 1e-06), (8, DH)
            )

    def forward(h):
        for i, buf in enumerate((kin, din)):
            j = 2 * h + i
            done("a2a", j)
            remote(buf.at[h, c], buf.at[h, c], fw_s.at[j], fw_r.at[j], tok=sib).start()
            track("fw", j, buf.at[h, c], buf.at[h, 1 - c], fw_s, fw_r)

    def hidden_grads(h, core):
        @pl.loop(0, SPAN // TILE)
        def _(step):
            at = pl.ds(pl.multiple_of(step * TILE, TILE), TILE)
            z = jnp.dot(kin[h, core, at, :], wb13[h], preferred_element_type=F32)
            dh = lax.dot_general(din[h, core, at, :], wb2[h], NT, preferred_element_type=F32)
            z1, z3 = z[:, :HALF], z[:, HALF:]
            sg = 1.0 / (1.0 + jnp.exp(-z1))
            act = z1 * sg
            hid[core, at, :] = (act * z3).astype(BF)
            dz[core, at, :HALF] = (dh * z3 * sg * (1.0 + z1 * (1.0 - sg))).astype(BF)
            dz[core, at, HALF:] = (dh * act).astype(BF)

    def send_y(src, land, rows, sems, i):
        for o, p in zip((1, 2, 3), ypeers):
            block = pl.ds(pl.multiple_of(lax.rem(y + o, 4) * rows, rows), rows)
            remote(src.at[block], land.at[pl.ds((3 - o) * rows, rows)], ry_s.at[i], ry_r.at[i], tok=p).start()
        track("ry", i, src.at[pl.ds(0, 3 * rows)], land, ry_s, ry_r)

    def weight_grads(h):
        g = lax.dot_general(kin[h, 0], dz[0], TN, preferred_element_type=F32)
        g += lax.dot_general(kin[h, 1], dz[1], TN, preferred_element_type=F32)
        gs13[h] = g.astype(BF)
        send_y(gs13.at[h], ry13.at[h], 128, ry_s, 2 * h)
        g = lax.dot_general(hid[0], din[h, 0], TN, preferred_element_type=F32)
        g += lax.dot_general(hid[1], din[h, 1], TN, preferred_element_type=F32)
        gs2[h] = g.astype(BF)
        send_y(gs2.at[h], ry2.at[h], 64, ry_s, 2 * h + 1)

    mats = ((gs13, ry13, py13, zs13, rz13, gg13, 128), (gs2, ry2, py2, zs2, rz2, gg2, 64))

    def reduce_y(h):
        for i, (gs, ry, py, zs, rz, gg, n) in enumerate(mats):
            done("ry", 2 * h + i)
            own = pl.ds(pl.multiple_of(y * n, n), n)
            total = gs[h, own, :].astype(F32)
            for o in range(3):
                total += ry[h, pl.ds(o * n, n), :].astype(F32)
            py[h] = total
            zs[h] = py[h, pl.ds(pl.multiple_of((1 - zh) * (n // 2), n // 2), n // 2), :].astype(BF)
            remote(zs.at[h], rz.at[h], rz_s.at[2 * h + i], rz_r.at[2 * h + i], tok=zpeer).start()
            track("rz", 2 * h + i, zs.at[h], rz.at[h], rz_s, rz_r)

    def gather(h):
        for i, (gs, ry, py, zs, rz, gg, n) in enumerate(mats):
            k = n // 2
            done("rz", 2 * h + i)
            total = py[h, pl.ds(pl.multiple_of(zh * k, k), k), :] + rz[h].astype(F32)
            own = pl.ds(pl.multiple_of(y * n + zh * k, k), k)
            gg[h, c, own, :] = total.astype(BF)
            view = gg.at[h, c, own]
            other = pl.ds(pl.multiple_of(y * n + (1 - zh) * k, k), k)
            remote(view, view, az_s.at[2 * h + i], az_r.at[2 * h + i], tok=zpeer).start()
            track("az", 2 * h + i, view, gg.at[h, c, other], az_s, az_r)
            for p in ypeers:
                remote(view, view, ay_s.at[2 * h + i], ay_r.at[2 * h + i], tok=p).start()

    def pass_on(h):
        for i, (gs, ry, py, zs, rz, gg, n) in enumerate(mats):
            k = n // 2
            other = pl.ds(pl.multiple_of(y * n + (1 - zh) * k, k), k)
            view = gg.at[h, c, other]
            done("az", 2 * h + i)
            for p in ypeers:
                remote(view, view, ay_s.at[2 * h + i], ay_r.at[2 * h + i], tok=p).start()
            three = gg.at[h, c, pl.ds(0, 3 * n)]
            track("ay", 2 * h + i, three, three, ay_s, ay_r)

    def share(h):
        for i, (gs, ry, py, zs, rz, gg, n) in enumerate(mats):
            j = 2 * h + i
            done("ay", j)
            remote(gg.at[h, c], gg.at[h, c], fg_s.at[j], fg_r.at[j], tok=sib).start()
            track("fg", j, gg.at[h, c], gg.at[h, 1 - c], fg_s, fg_r)

    outs = (out1, out3, out2)

    def newton(h, m):
        def g_part(part):
            if m == 2:
                return gg2[h, part].astype(F32)
            return gg13[h, part, :, m * HALF : (m + 1) * HALF].astype(F32)

        squares = jnp.sum(g_part(0) ** 2) + jnp.sum(g_part(1) ** 2)
        scale = 1.0 / (jnp.sqrt(jnp.full((8, 128), squares, F32)) + 1e-06)
        scale = scale[:1, :1]
        for part in range(2):
            piece = g_part(part) * scale
            where = pl.ds(part * HALF, HALF)
            if m == 2:
                xs[where, :] = piece
                xb[0, where, :] = piece.astype(BF)
            else:
                xs[:, where] = piece
                xb[0, :, where] = piece.astype(BF)
        for step in range(ITERS):
            now, later = step % 2, (step + 1) % 2

            square = lax.dot_general(xb[now], xb[now], NT, preferred_element_type=F32)
            cube = jnp.dot(square.astype(BF), xb[now], preferred_element_type=F32)
            fresh = 1.5 * xs[...] - 0.5 * cube
            xs[...] = fresh
            if step < ITERS - 1:
                xb[later] = fresh.astype(BF)

        update = wv[m, h] - xs[...]
        new_norm = jnp.sqrt(jnp.sum(update * update, axis=0, keepdims=True) + 1e-06)
        fresh = update * (oldn[3 * h + m, :1, :] / new_norm)
        nf[h, m] = fresh
        pltpu.make_async_copy(nf.at[h, m], outs[m].at[h], nf_sem.at[3 * h + m]).start()
        pending["nf_s", 3 * h + m] = (nf.at[h, m], nf_sem.at[3 * h + m])
        nb[m] = fresh.astype(BF)

    def apply(h):
        done("a2a", 4 + h)

        for tile in range(SPAN // TILE):
            at = pl.ds(tile * TILE, TILE)
            q = qin[h, at, :]
            y1 = jnp.dot(q, nb[0], preferred_element_type=F32)
            y3 = jnp.dot(q, nb[1], preferred_element_type=F32)
            qh[...] = (y1 * (1.0 / (1.0 + jnp.exp(-y1))) * y3).astype(BF)
            ov[h, at, :] = jnp.dot(qh[...], nb[2], preferred_element_type=F32).astype(BF)
            for i in range(tile * TILE // ROWS, (tile + 1) * TILE // ROWS):
                land = mixed.at[:, columns(hi, h)]
                if i == OWN:
                    pltpu.make_async_copy(ov.at[h, slot(i)], land, o_r.at[h]).start()
                else:
                    remote(ov.at[h, slot(i)], land, o_s.at[h], o_r.at[h], head=peers[i]).start()
        track("out", h, ov.at[h, pl.ds(0, SPAN - ROWS)], ov.at[h], o_s, o_r)

    def arrived(name, h):
        done(name, 2 * h)
        done(name, 2 * h + 1)

    steps = [
        lambda: forward(0),
        lambda: hidden_grads(0, c),
        lambda: arrived("fw", 0),
        lambda: hidden_grads(0, 1 - c),
        lambda: weight_grads(0),
        lambda: forward(1),
        lambda: hidden_grads(1, c),
        lambda: arrived("fw", 1),
        lambda: hidden_grads(1, 1 - c),
        lambda: weight_grads(1),
        lambda: scatter(q_hbm, qin.at[0], 4, 0),
        lambda: scatter(q_hbm, qin.at[1], 5, 1),
        lambda: reduce_y(0),
        lambda: gather(0),
        lambda: pass_on(0),
        lambda: reduce_y(1),
        lambda: gather(1),
        lambda: pass_on(1),
        lambda: share(0),
        lambda: arrived("fg", 0),
        lambda: newton(0, 0),
        lambda: newton(0, 1),
        lambda: newton(0, 2),
        lambda: share(1),
        lambda: apply(0),
        lambda: arrived("fg", 1),
        lambda: newton(1, 0),
        lambda: newton(1, 1),
        lambda: newton(1, 2),
        lambda: apply(1),
    ]
    for step in steps:
        step()

    for key in sorted(pending, key=lambda key: (key[0].endswith("_s"), key)):
        done(*key)


def hand_out(*refs):
    count = len(refs) // 2
    copies = [pltpu.make_async_copy(refs[i], refs[count + i], refs[-1].at[i]) for i in range(count)]
    for copy in copies:
        copy.start()
    for copy in copies:
        copy.wait()


def on_device(queries, keys, values, rates, w_first, w_gate, w_second):
    any_spec = pl.BlockSpec(memory_space=pl.ANY)
    dma = pltpu.SemaphoreType.DMA
    weights = jax.ShapeDtypeStruct(w_first.shape, F32)
    vm = pltpu.VMEM
    results = pl.pallas_call(
        kernel,
        out_shape=(jax.ShapeDtypeStruct(queries.shape, BF), weights, weights, weights),
        in_specs=[any_spec] * 7,
        out_specs=[any_spec] * 4,
        scratch_shapes=[
            vm((3, 2, DH, DH), F32),
            vm(values.shape, BF),
            vm(rates.shape[::-1], BF),
            vm(values.shape, BF),
            vm((2, 2, SPAN, DH), BF),
            vm((2, 2, SPAN, DH), BF),
            vm((2, SPAN, DH), BF),
            vm((2, DH, DH), BF),
            vm((2, HALF, DH), BF),
            vm((6, 8, DH), F32),
            vm((2, SPAN, DH), BF),
            vm((2, SPAN, HALF), BF),
            vm((2, DH, DH), BF),
            vm((2, HALF, DH), BF),
            vm((2, 384, DH), BF),
            vm((2, 192, DH), BF),
            vm((2, 128, DH), F32),
            vm((2, 64, DH), F32),
            vm((2, 64, DH), BF),
            vm((2, 32, DH), BF),
            vm((2, 64, DH), BF),
            vm((2, 32, DH), BF),
            vm((2, 2, DH, DH), BF),
            vm((2, 2, HALF, DH), BF),
            vm((DH, DH), F32),
            vm((2, DH, DH), BF),
            vm((3, DH, DH), BF),
            vm((TILE, DH), BF),
            vm((2, SPAN, DH), BF),
            vm((2, 3, DH, DH), F32),
            dma((5,)), dma((6,)), dma((6,)), dma((4,)), dma((4,)), dma((4,)), dma((4,)),
            dma((4,)), dma((4,)), dma((4,)), dma((4,)), dma((4,)), dma((4,)), dma((4,)),
            dma((4,)), dma((2,)), dma((2,)), dma((6,)),
        ],
        compiler_params=pltpu.CompilerParams(
            collective_id=0, has_side_effects=True, vmem_limit_bytes=VMEM_BYTES
        ),
        name="layer",
    )(queries, keys, values, rates.T, w_first, w_gate, w_second)
    return pl.pallas_call(
        hand_out,
        out_shape=(jax.ShapeDtypeStruct(queries.shape, BF), weights, weights, weights),
        in_specs=[any_spec] * 4,
        out_specs=[any_spec] * 4,
        scratch_shapes=[dma((4,))],
        name="hand_out",
    )(*results)


def solution(mesh):
    placed = (
        P(("head", "tok"), None),
        P(("head", "tok"), None),
        P(("head", "tok"), None),
        P(("head", "tok"), None),
        P("head", None, None),
        P("head", None, None),
        P("head", None, None),
    )
    return jax.shard_map(
        on_device,
        mesh=mesh,
        in_specs=placed,
        out_specs=(
            P(("head", "tok"), None),
            P("head", None, None),
            P("head", None, None),
            P("head", None, None),
        ),
        check_vma=False,
    )
```

time: 114 us -> 315 us (2.76)
  Pallas kernels: 103 us -> 314 us
  local copies, waits for them, and re-layouts: 9.8 us -> 0 us
    pallas_call x0 -> x1, Pallas kernels: none -> 223 us  [on_device(): pl.pallas_call(hand_out, out_shape=(jax.ShapeDtypeStruct(queries.shape, B...]
    pallas_call x1, Pallas kernels: 103 us -> 90.5 us  [on_device(): pl.pallas_call(kernel, out_shape=(jax.ShapeDtypeStruct(queries.shape, BF)...]
    unnamed x11 -> x0, local copies, waits for them, and re-layouts: 9.8 us -> none
where the time goes in v1:
time: 315 us
  Pallas kernels  314 us (100%)
    pallas_call x1, Pallas kernels, on_device(): pl.pallas_call(hand_out, out_shape=(jax.ShapeDtypeStruct(queries.shape, B...  223 us
    pallas_call x1, Pallas kernels, on_device(): pl.pallas_call(kernel, out_shape=(jax.ShapeDtypeStruct(queries.shape, BF)...  90.5 us

profile of v1, /device:TPU:1, one launch (start us, length us, event | category | flops | bytes accessed | tf_op | source)
XLA Modules:
  0.0 314.9 jit_solution(3031736787207724649)
XLA Ops:
  0.6 90.5 %layer.1 = (bf16[64,8192]{1,0:T(8,128)(2,1)}, f32[2,512,512]{2,1,0:T(8,128)}, f32[2,512,512]{2,1,0:T(8,128)}, f32[2,512,512]{2,1,0:T(8,128)}) custom-call(bf16[64,8192]{1,0:T(8,128)(2,1)} %q_hbm.1, bf16[64,8192]{1,0:T(8,128)(2,1)} %k_hbm.1, bf16[64,8192]{1,0:T(8,128)(2,1)} %v_hbm.1, bf16[16,64]{1,0:T(8,128)(2,1)} %bitcast.1, f32[2,512,512]{2,1,0:T(8,128)} %w1_hbm.1, ...), custom_call_target="tpu_custom_call" | custom-call | tf_op jit(solution)/shard_map/layer/pallas_call | solution.py:310
  91.2 223.5 %hand_out.1 = (bf16[64,8192]{1,0:T(8,128)(2,1)}, f32[2,512,512]{2,1,0:T(8,128)}, f32[2,512,512]{2,1,0:T(8,128)}, f32[2,512,512]{2,1,0:T(8,128)}) custom-call(bf16[64,8192]{1,0:T(8,128)(2,1)} %get-tuple-element.8.refs_0_, f32[2,512,512]{2,1,0:T(8,128)} %get-tuple-element.9.refs_1_, f32[2,512,512]{2,1,0:T(8,128)} %get-tuple-element.10.refs_2_, ...), custom_call_target="tpu_custom_call" | custom-call | tf_op jit(solution)/shard_map/hand_out/pallas_call | solution.py:355

commit v2 on v1

--- a/solution.py
+++ b/solution.py
@@ -29,17 +29,17 @@
     q_hbm, k_hbm, v_hbm, r_hbm, w1_hbm, w3_hbm, w2_hbm,
     mixed, out1, out3, out2,
     wv, vv, rv, dv, kin, din, qin, wb13, wb2, oldn, dz, hid,
-    gs13, gs2, ry13, ry2, py13, py2, zs13, zs2, rz13, rz2, gg13, gg2,
-    xs, xb, nb, qh, ov, nf,
-    load_sem, a2a_s, a2a_r, fw_s, fw_r, ry_s, ry_r, rz_s, rz_r,
-    az_s, az_r, ay_s, ay_r, fg_s, fg_r, o_s, o_r, nf_sem,
+    gs13, gs2, ra13, ra2, rb13, rb2, ry13, ry2, py13, py2, zs13, zs2, rz13, rz2, gg13, gg2,
+    xs, xb, xf, nb, qh, ov, nf,
+    load_sem, a2a_s, a2a_r, fw_s, fw_r, ra_r, ry_s, ry_r, rz_s, rz_r,
+    az_s, az_r, ay_s, ay_r, au_r, ad_r, fg_s, fg_r, xf_s, xf_r, o_s, o_r, nf_sem,
 ):
     hi = lax.axis_index("head")
     tk = lax.axis_index("tok")
     x, zl = hi // 2, lax.rem(hi, 2)
     zh, y, c = tk // 8, lax.rem(tk // 2, 4), lax.rem(tk, 2)
     peers = [lax.rem(x + dx, 4) * 2 + lax.rem(zl + dz_, 2) for dx, dz_ in OFFSETS]
-    ypeers = [zh * 8 + lax.rem(y + o, 4) * 2 + c for o in (1, 2, 3)]
+    up, down = [zh * 8 + lax.rem(y + o, 4) * 2 + c for o in (1, 3)]
     zpeer = (1 - zh) * 8 + y * 2 + c
     sib = zh * 8 + y * 2 + (1 - c)
 
@@ -68,9 +68,9 @@
     barrier = pltpu.get_barrier_semaphore()
     for p in peers:
         pl.semaphore_signal(barrier, inc=1, device_id={"head": p}, device_id_type=MESH)
-    for p in ypeers + [zpeer, sib]:
+    for p in (up, down, zpeer, sib):
         pl.semaphore_signal(barrier, inc=1, device_id={"tok": p}, device_id_type=MESH)
-    pl.semaphore_wait(barrier, len(peers) + 5)
+    pl.semaphore_wait(barrier, len(peers) + 4)
 
     def slot(i):
         return pl.ds(i * ROWS, ROWS)
@@ -108,7 +108,7 @@
         wb2[h] = wv[2, h, half, :].astype(BF)
         for m in range(3):
             w = wv[m, h]
-            oldn[3 * h + m] = jnp.broadcast_to(
+            oldn[h, m] = jnp.broadcast_to(
                 jnp.sqrt(jnp.sum(w * w, axis=0, keepdims=True) + 1e-06), (8, DH)
             )
 
@@ -132,105 +132,147 @@
             dz[core, at, :HALF] = (dh * z3 * sg * (1.0 + z1 * (1.0 - sg))).astype(BF)
             dz[core, at, HALF:] = (dh * act).astype(BF)
 
-    def send_y(src, land, rows, sems, i):
-        for o, p in zip((1, 2, 3), ypeers):
-            block = pl.ds(pl.multiple_of(lax.rem(y + o, 4) * rows, rows), rows)
-            remote(src.at[block], land.at[pl.ds((3 - o) * rows, rows)], ry_s.at[i], ry_r.at[i], tok=p).start()
-        track("ry", i, src.at[pl.ds(0, 3 * rows)], land, ry_s, ry_r)
+    def block(j, rows, start=0, count=None):
+        return pl.ds(pl.multiple_of(lax.rem(y + j, 4) * rows + start, 16), count or rows)
+
+    def send_y(gs, ra, ry, n, i):
+        k = n // 2
+        remote(gs.at[block(2, n, 0, k)], ra.at[0], ry_s.at[i], ra_r.at[i], tok=up).start()
+        remote(gs.at[block(2, n, k, k)], ra.at[1], ry_s.at[i], ra_r.at[i], tok=down).start()
+        remote(gs.at[block(1, n, k, k)], ry.at[0], ry_s.at[i], ry_r.at[i], tok=up).start()
+        remote(gs.at[block(3, n, 0, k)], ry.at[1], ry_s.at[i], ry_r.at[i], tok=down).start()
+        pending["ra", i] = (ra, ra_r.at[i])
 
     def weight_grads(h):
         g = lax.dot_general(kin[h, 0], dz[0], TN, preferred_element_type=F32)
         g += lax.dot_general(kin[h, 1], dz[1], TN, preferred_element_type=F32)
         gs13[h] = g.astype(BF)
-        send_y(gs13.at[h], ry13.at[h], 128, ry_s, 2 * h)
+        send_y(gs13.at[h], ra13.at[h], ry13.at[h], 128, 2 * h)
         g = lax.dot_general(hid[0], din[h, 0], TN, preferred_element_type=F32)
         g += lax.dot_general(hid[1], din[h, 1], TN, preferred_element_type=F32)
         gs2[h] = g.astype(BF)
-        send_y(gs2.at[h], ry2.at[h], 64, ry_s, 2 * h + 1)
-
-    mats = ((gs13, ry13, py13, zs13, rz13, gg13, 128), (gs2, ry2, py2, zs2, rz2, gg2, 64))
+        send_y(gs2.at[h], ra2.at[h], ry2.at[h], 64, 2 * h + 1)
+
+    mats = (
+        (gs13, ra13, rb13, ry13, py13, zs13, rz13, gg13, 128),
+        (gs2, ra2, rb2, ry2, py2, zs2, rz2, gg2, 64),
+    )
+
+    def relay_y(h):
+        for i, (gs, ra, rb, ry, py, zs, rz, gg, n) in enumerate(mats):
+            j, k = 2 * h + i, n // 2
+            done("ra", j)
+            rb[h, 0] = (gs[h, block(1, n, 0, k), :].astype(F32) + ra[h, 0].astype(F32)).astype(BF)
+            rb[h, 1] = (gs[h, block(3, n, k, k), :].astype(F32) + ra[h, 1].astype(F32)).astype(BF)
+            remote(rb.at[h, 0], ry.at[h, 2], ry_s.at[j], ry_r.at[j], tok=up).start()
+            remote(rb.at[h, 1], ry.at[h, 3], ry_s.at[j], ry_r.at[j], tok=down).start()
+            track("ry", j, gs.at[h, pl.ds(0, 3 * n)], ry.at[h], ry_s, ry_r)
 
     def reduce_y(h):
-        for i, (gs, ry, py, zs, rz, gg, n) in enumerate(mats):
-            done("ry", 2 * h + i)
-            own = pl.ds(pl.multiple_of(y * n, n), n)
-            total = gs[h, own, :].astype(F32)
-            for o in range(3):
-                total += ry[h, pl.ds(o * n, n), :].astype(F32)
-            py[h] = total
-            zs[h] = py[h, pl.ds(pl.multiple_of((1 - zh) * (n // 2), n // 2), n // 2), :].astype(BF)
-            remote(zs.at[h], rz.at[h], rz_s.at[2 * h + i], rz_r.at[2 * h + i], tok=zpeer).start()
-            track("rz", 2 * h + i, zs.at[h], rz.at[h], rz_s, rz_r)
+        for i, (gs, ra, rb, ry, py, zs, rz, gg, n) in enumerate(mats):
+            j, k = 2 * h + i, n // 2
+            done("ry", j)
+            own = gs[h, block(0, n), :].astype(F32)
+            py[h, :k, :] = own[:k] + (ry[h, 2].astype(F32) + ry[h, 1].astype(F32))
+            py[h, k:, :] = own[k:] + (ry[h, 0].astype(F32) + ry[h, 3].astype(F32))
+            zs[h] = py[h, pl.ds(pl.multiple_of((1 - zh) * k, k), k), :].astype(BF)
+            remote(zs.at[h], rz.at[h], rz_s.at[j], rz_r.at[j], tok=zpeer).start()
+            track("rz", j, zs.at[h], rz.at[h], rz_s, rz_r)
+
+    def piece(gg, h, j, n, e):
+        k = n // 2
+        return gg.at[h, c, pl.ds(pl.multiple_of(lax.rem(y + j, 4) * n + e * k, k), k)]
 
     def gather(h):
-        for i, (gs, ry, py, zs, rz, gg, n) in enumerate(mats):
-            k = n // 2
-            done("rz", 2 * h + i)
+        for i, (gs, ra, rb, ry, py, zs, rz, gg, n) in enumerate(mats):
+            j, k = 2 * h + i, n // 2
+            done("rz", j)
             total = py[h, pl.ds(pl.multiple_of(zh * k, k), k), :] + rz[h].astype(F32)
-            own = pl.ds(pl.multiple_of(y * n + zh * k, k), k)
-            gg[h, c, own, :] = total.astype(BF)
-            view = gg.at[h, c, own]
-            other = pl.ds(pl.multiple_of(y * n + (1 - zh) * k, k), k)
-            remote(view, view, az_s.at[2 * h + i], az_r.at[2 * h + i], tok=zpeer).start()
-            track("az", 2 * h + i, view, gg.at[h, c, other], az_s, az_r)
-            for p in ypeers:
-                remote(view, view, ay_s.at[2 * h + i], ay_r.at[2 * h + i], tok=p).start()
+            view = piece(gg, h, 0, n, zh)
+            view[...] = total.astype(BF)
+            remote(view, view, az_s.at[j], az_r.at[j], tok=zpeer).start()
+            remote(view, view, ay_s.at[j], au_r.at[j], tok=up).start()
+            remote(view, view, ay_s.at[j], ay_r.at[j], tok=down).start()
+            track("az", j, view, piece(gg, h, 0, n, 1 - zh), az_s, az_r)
 
     def pass_on(h):
-        for i, (gs, ry, py, zs, rz, gg, n) in enumerate(mats):
-            k = n // 2
-            other = pl.ds(pl.multiple_of(y * n + (1 - zh) * k, k), k)
-            view = gg.at[h, c, other]
-            done("az", 2 * h + i)
-            for p in ypeers:
-                remote(view, view, ay_s.at[2 * h + i], ay_r.at[2 * h + i], tok=p).start()
+        for i, (gs, ra, rb, ry, py, zs, rz, gg, n) in enumerate(mats):
+            j = 2 * h + i
+            done("az", j)
+            view = piece(gg, h, 0, n, 1 - zh)
+            remote(view, view, ay_s.at[j], ad_r.at[j], tok=down).start()
+            remote(view, view, ay_s.at[j], ay_r.at[j], tok=up).start()
+
+    def relay_gather(h):
+        for i, (gs, ra, rb, ry, py, zs, rz, gg, n) in enumerate(mats):
+            j = 2 * h + i
+            for sem, near, e, to in ((au_r, 3, zh, up), (ad_r, 1, 1 - zh, down)):
+                view = piece(gg, h, near, n, e)
+                pltpu.make_async_copy(view, view, sem.at[j]).wait()
+                remote(view, view, ay_s.at[j], ay_r.at[j], tok=to).start()
             three = gg.at[h, c, pl.ds(0, 3 * n)]
-            track("ay", 2 * h + i, three, three, ay_s, ay_r)
+            track("ay", j, three, gg.at[h, c, pl.ds(0, 2 * n)], ay_s, ay_r)
 
     def share(h):
-        for i, (gs, ry, py, zs, rz, gg, n) in enumerate(mats):
-            j = 2 * h + i
-            done("ay", j)
-            remote(gg.at[h, c], gg.at[h, c], fg_s.at[j], fg_r.at[j], tok=sib).start()
-            track("fg", j, gg.at[h, c], gg.at[h, 1 - c], fg_s, fg_r)
+        done("ay", 2 * h)
+        mine = gg13.at[h, c, :, pl.ds(pl.multiple_of((1 - c) * HALF, HALF), HALF)]
+        theirs = gg13.at[h, 1 - c, :, half]
+        remote(mine, mine, fg_s.at[2 * h], fg_r.at[2 * h], tok=sib).start()
+        track("fg", 2 * h, mine, theirs, fg_s, fg_r)
+        done("ay", 2 * h + 1)
+        remote(gg2.at[h, c], gg2.at[h, c], fg_s.at[2 * h + 1], fg_r.at[2 * h + 1], tok=sib).start()
+        track("fg", 2 * h + 1, gg2.at[h, c], gg2.at[h, 1 - c], fg_s, fg_r)
 
     outs = (out1, out3, out2)
 
-    def newton(h, m):
-        def g_part(part):
-            if m == 2:
-                return gg2[h, part].astype(F32)
-            return gg13[h, part, :, m * HALF : (m + 1) * HALF].astype(F32)
-
-        squares = jnp.sum(g_part(0) ** 2) + jnp.sum(g_part(1) ** 2)
+    def newton(parts):
+        squares = jnp.sum(parts[0] ** 2) + jnp.sum(parts[1] ** 2)
         scale = 1.0 / (jnp.sqrt(jnp.full((8, 128), squares, F32)) + 1e-06)
         scale = scale[:1, :1]
         for part in range(2):
-            piece = g_part(part) * scale
+            piece_ = parts[part] * scale
             where = pl.ds(part * HALF, HALF)
-            if m == 2:
-                xs[where, :] = piece
-                xb[0, where, :] = piece.astype(BF)
+            if parts[part].shape[0] == HALF:
+                xs[where, :] = piece_
+                xb[0, where, :] = piece_.astype(BF)
             else:
-                xs[:, where] = piece
-                xb[0, :, where] = piece.astype(BF)
+                xs[:, where] = piece_
+                xb[0, :, where] = piece_.astype(BF)
         for step in range(ITERS):
             now, later = step % 2, (step + 1) % 2
-
             square = lax.dot_general(xb[now], xb[now], NT, preferred_element_type=F32)
             cube = jnp.dot(square.astype(BF), xb[now], preferred_element_type=F32)
             fresh = 1.5 * xs[...] - 0.5 * cube
-            xs[...] = fresh
             if step < ITERS - 1:
+                xs[...] = fresh
                 xb[later] = fresh.astype(BF)
-
-        update = wv[m, h] - xs[...]
+        return fresh
+
+    def renew(h, m, ortho):
+        update = wv[m, h] - ortho
         new_norm = jnp.sqrt(jnp.sum(update * update, axis=0, keepdims=True) + 1e-06)
-        fresh = update * (oldn[3 * h + m, :1, :] / new_norm)
+        fresh = update * (oldn[h, m, :1, :] / new_norm)
         nf[h, m] = fresh
-        pltpu.make_async_copy(nf.at[h, m], outs[m].at[h], nf_sem.at[3 * h + m]).start()
-        pending["nf_s", 3 * h + m] = (nf.at[h, m], nf_sem.at[3 * h + m])
         nb[m] = fresh.astype(BF)
+
+    def newton_own(h):
+        done("fg", 2 * h)
+        xf[h, c] = newton([gg13[h, part, :, half].astype(F32) for part in range(2)]).astype(BF)
+        remote(xf.at[h, c], xf.at[h, c], xf_s.at[h], xf_r.at[h], tok=sib).start()
+        track("xf", h, xf.at[h, c], xf.at[h, 1 - c], xf_s, xf_r)
+
+    def newton_second(h):
+        done("fg", 2 * h + 1)
+        renew(h, 2, newton([gg2[h, part].astype(F32) for part in range(2)]))
+
+    def renew_both(h):
+        renew(h, c, xf[h, c].astype(F32))
+        done("xf", h)
+        renew(h, 1 - c, xf[h, 1 - c].astype(F32))
+        for m in range(3):
+            sem = nf_sem.at[3 * h + m]
+            pltpu.make_async_copy(nf.at[h, m], outs[m].at[h], sem).start()
+            pending["nf_s", 3 * h + m] = (nf.at[h, m], sem)
 
     def apply(h):
         done("a2a", 4 + h)
@@ -260,30 +302,25 @@
         lambda: arrived("fw", 0),
         lambda: hidden_grads(0, 1 - c),
         lambda: weight_grads(0),
+        lambda: relay_y(0),
         lambda: forward(1),
         lambda: hidden_grads(1, c),
         lambda: arrived("fw", 1),
         lambda: hidden_grads(1, 1 - c),
         lambda: weight_grads(1),
-        lambda: scatter(q_hbm, qin.at[0], 4, 0),
-        lambda: scatter(q_hbm, qin.at[1], 5, 1),
         lambda: reduce_y(0),
-        lambda: gather(0),
-        lambda: pass_on(0),
+        lambda: relay_y(1),
+        lambda: [scatter(q_hbm, qin.at[h], 4 + h, h) for h in range(2)],
+        lambda: [gather(0), pass_on(0), relay_gather(0)],
         lambda: reduce_y(1),
-        lambda: gather(1),
-        lambda: pass_on(1),
-        lambda: share(0),
-        lambda: arrived("fg", 0),
-        lambda: newton(0, 0),
-        lambda: newton(0, 1),
-        lambda: newton(0, 2),
+        lambda: [share(0), gather(1), newton_own(0), pass_on(1), relay_gather(1)],
+        lambda: newton_second(0),
+        lambda: renew_both(0),
         lambda: share(1),
         lambda: apply(0),
-        lambda: arrived("fg", 1),
-        lambda: newton(1, 0),
-        lambda: newton(1, 1),
-        lambda: newton(1, 2),
+        lambda: newton_own(1),
+        lambda: newton_second(1),
+        lambda: renew_both(1),
         lambda: apply(1),
     ]
     for step in steps:
@@ -294,12 +331,25 @@
 
 
 def hand_out(*refs):
-    count = len(refs) // 2
-    copies = [pltpu.make_async_copy(refs[i], refs[count + i], refs[-1].at[i]) for i in range(count)]
-    for copy in copies:
-        copy.start()
-    for copy in copies:
-        copy.wait()
+    ins, outs, held, in_sem, out_sem = refs[:4], refs[4:8], refs[8:12], refs[12], refs[13]
+    parts = [(0, None)] + [(i, h) for h in range(2) for i in (1, 2, 3)]
+
+    def view(ref, h):
+        return ref if h is None else ref.at[h]
+
+    loads = [
+        pltpu.make_async_copy(view(ins[i], h), view(held[i], h), in_sem.at[n]) for n, (i, h) in enumerate(parts)
+    ]
+    stores = [
+        pltpu.make_async_copy(view(held[i], h), view(outs[i], h), out_sem.at[n]) for n, (i, h) in enumerate(parts)
+    ]
+    for load in loads:
+        load.start()
+    for load, store in zip(loads, stores):
+        load.wait()
+        store.start()
+    for store in stores:
+        store.wait()
 
 
 def on_device(queries, keys, values, rates, w_first, w_gate, w_second):
@@ -322,13 +372,17 @@
             vm((2, SPAN, DH), BF),
             vm((2, DH, DH), BF),
             vm((2, HALF, DH), BF),
-            vm((6, 8, DH), F32),
+            vm((2, 3, 8, DH), F32),
             vm((2, SPAN, DH), BF),
             vm((2, SPAN, HALF), BF),
             vm((2, DH, DH), BF),
             vm((2, HALF, DH), BF),
-            vm((2, 384, DH), BF),
-            vm((2, 192, DH), BF),
+            vm((2, 2, 64, DH), BF),
+            vm((2, 2, 32, DH), BF),
+            vm((2, 2, 64, DH), BF),
+            vm((2, 2, 32, DH), BF),
+            vm((2, 4, 64, DH), BF),
+            vm((2, 4, 32, DH), BF),
             vm((2, 128, DH), F32),
             vm((2, 64, DH), F32),
             vm((2, 64, DH), BF),
@@ -339,13 +393,14 @@
             vm((2, 2, HALF, DH), BF),
             vm((DH, DH), F32),
             vm((2, DH, DH), BF),
+            vm((2, 2, DH, DH), BF),
             vm((3, DH, DH), BF),
             vm((TILE, DH), BF),
             vm((2, SPAN, DH), BF),
             vm((2, 3, DH, DH), F32),
-            dma((5,)), dma((6,)), dma((6,)), dma((4,)), dma((4,)), dma((4,)), dma((4,)),
-            dma((4,)), dma((4,)), dma((4,)), dma((4,)), dma((4,)), dma((4,)), dma((4,)),
-            dma((4,)), dma((2,)), dma((2,)), dma((6,)),
+            dma((5,)), dma((6,)), dma((6,)), dma((4,)), dma((4,)), dma((4,)), dma((4,)), dma((4,)),
+            dma((4,)), dma((4,)), dma((4,)), dma((4,)), dma((4,)), dma((4,)), dma((4,)), dma((4,)),
+            dma((4,)), dma((4,)), dma((2,)), dma((2,)), dma((2,)), dma((2,)), dma((6,)),
         ],
         compiler_params=pltpu.CompilerParams(
             collective_id=0, has_side_effects=True, vmem_limit_bytes=VMEM_BYTES
@@ -357,7 +412,8 @@
         out_shape=(jax.ShapeDtypeStruct(queries.shape, BF), weights, weights, weights),
         in_specs=[any_spec] * 4,
         out_specs=[any_spec] * 4,
-        scratch_shapes=[dma((4,))],
+        scratch_shapes=[vm(queries.shape, BF)] + [vm(w_first.shape, F32)] * 3 + [dma((7,)), dma((7,))],
+        compiler_params=pltpu.CompilerParams(vmem_limit_bytes=VMEM_BYTES),
         name="hand_out",
     )(*results)
 

time: 315 us -> 101 us (0.32)
  Pallas kernels: 314 us -> 99.9 us
    pallas_call x1, Pallas kernels: 223 us -> 6.06 us  [on_device(): pl.pallas_call(hand_out, out_shape=(jax.ShapeDtypeStruct(queries.shape, B...]
    pallas_call x1, Pallas kernels: 90.5 us -> 93.8 us  [on_device(): pl.pallas_call(kernel, out_shape=(jax.ShapeDtypeStruct(queries.shape, BF)...]
where the time goes in v2:
time: 101 us
  Pallas kernels  99.9 us (99%)
    pallas_call x1, Pallas kernels, on_device(): pl.pallas_call(kernel, out_shape=(jax.ShapeDtypeStruct(queries.shape, BF)...  93.8 us
    pallas_call x1, Pallas kernels, on_device(): pl.pallas_call(hand_out, out_shape=(jax.ShapeDtypeStruct(queries.shape, B...  6.06 us

profile of v2, /device:TPU:1, one launch (start us, length us, event | category | flops | bytes accessed | tf_op | source)
XLA Modules:
  0.0 100.7 jit_solution(5125199000872633056)
XLA Ops:
  0.6 93.8 %layer.1 = (bf16[64,8192]{1,0:T(8,128)(2,1)}, f32[2,512,512]{2,1,0:T(8,128)}, f32[2,512,512]{2,1,0:T(8,128)}, f32[2,512,512]{2,1,0:T(8,128)}) custom-call(bf16[64,8192]{1,0:T(8,128)(2,1)} %q_hbm.1, bf16[64,8192]{1,0:T(8,128)(2,1)} %k_hbm.1, bf16[64,8192]{1,0:T(8,128)(2,1)} %v_hbm.1, bf16[16,64]{1,0:T(8,128)(2,1)} %bitcast.1, f32[2,512,512]{2,1,0:T(8,128)} %w1_hbm.1, ...), custom_call_target="tpu_custom_call" | custom-call | tf_op jit(solution)/shard_map/layer/pallas_call | solution.py:360
  94.5 6.1 %hand_out.1 = (bf16[64,8192]{1,0:T(8,128)(2,1)}, f32[2,512,512]{2,1,0:T(8,128)}, f32[2,512,512]{2,1,0:T(8,128)}, f32[2,512,512]{2,1,0:T(8,128)}) custom-call(bf16[64,8192]{1,0:T(8,128)(2,1)} %get-tuple-element.8.refs_0_, f32[2,512,512]{2,1,0:T(8,128)} %get-tuple-element.9.refs_1_, f32[2,512,512]{2,1,0:T(8,128)} %get-tuple-element.10.refs_2_, ...), custom_call_target="tpu_custom_call" | custom-call | tf_op jit(solution)/shard_map/hand_out/pallas_call | solution.py:410

commit v3 on v2

--- a/solution.py
+++ b/solution.py
@@ -58,6 +58,12 @@
         pending[name + "_s", i] = (sent, send_sems.at[i])
         pending[name, i] = (arriving, recv_sems.at[i])
 
+    barrier = pltpu.get_barrier_semaphore()
+    for p in peers:
+        pl.semaphore_signal(barrier, inc=1, device_id={"head": p}, device_id_type=MESH)
+    for p in (up, down, zpeer, sib):
+        pl.semaphore_signal(barrier, inc=1, device_id={"tok": p}, device_id_type=MESH)
+
     loads = [pltpu.make_async_copy(v_hbm, vv, load_sem.at[0]), pltpu.make_async_copy(r_hbm, rv, load_sem.at[1])]
     loads += [
         pltpu.make_async_copy(w, wv.at[m], load_sem.at[2 + m]) for m, w in enumerate((w1_hbm, w3_hbm, w2_hbm))
@@ -65,11 +71,6 @@
     for copy in loads:
         copy.start()
 
-    barrier = pltpu.get_barrier_semaphore()
-    for p in peers:
-        pl.semaphore_signal(barrier, inc=1, device_id={"head": p}, device_id_type=MESH)
-    for p in (up, down, zpeer, sib):
-        pl.semaphore_signal(barrier, inc=1, device_id={"tok": p}, device_id_type=MESH)
     pl.semaphore_wait(barrier, len(peers) + 4)
 
     def slot(i):
@@ -304,19 +305,26 @@
         lambda: weight_grads(0),
         lambda: relay_y(0),
         lambda: forward(1),
+        lambda: scatter(q_hbm, qin.at[0], 4 + 0, 0),
         lambda: hidden_grads(1, c),
+        lambda: reduce_y(0),
         lambda: arrived("fw", 1),
         lambda: hidden_grads(1, 1 - c),
         lambda: weight_grads(1),
-        lambda: reduce_y(0),
+        lambda: gather(0),
         lambda: relay_y(1),
-        lambda: [scatter(q_hbm, qin.at[h], 4 + h, h) for h in range(2)],
-        lambda: [gather(0), pass_on(0), relay_gather(0)],
         lambda: reduce_y(1),
-        lambda: [share(0), gather(1), newton_own(0), pass_on(1), relay_gather(1)],
+        lambda: pass_on(0),
+        lambda: relay_gather(0),
+        lambda: gather(1),
+        lambda: pass_on(1),
+        lambda: share(0),
+        lambda: relay_gather(1),
+        lambda: newton_own(0),
+        lambda: share(1),
+        lambda: scatter(q_hbm, qin.at[1], 4 + 1, 1),
         lambda: newton_second(0),
         lambda: renew_both(0),
-        lambda: share(1),
         lambda: apply(0),
         lambda: newton_own(1),
         lambda: newton_second(1),
@@ -332,16 +340,19 @@
 
 def hand_out(*refs):
     ins, outs, held, in_sem, out_sem = refs[:4], refs[4:8], refs[8:12], refs[12], refs[13]
-    parts = [(0, None)] + [(i, h) for h in range(2) for i in (1, 2, 3)]
-
-    def view(ref, h):
-        return ref if h is None else ref.at[h]
+    parts = [(i, 0, row) for i in (1, 2, 3) for row in (0, HALF)]
+    parts += [(0, 0, 0)] + [(i, 1, row) for i in (1, 2, 3) for row in (0, HALF)]
+
+    def view(i, ref, h, row):
+        return ref.at[h, pl.ds(row, HALF)] if i else ref
 
     loads = [
-        pltpu.make_async_copy(view(ins[i], h), view(held[i], h), in_sem.at[n]) for n, (i, h) in enumerate(parts)
+        pltpu.make_async_copy(view(i, ins[i], h, r), view(i, held[i], h, r), in_sem.at[n])
+        for n, (i, h, r) in enumerate(parts)
     ]
     stores = [
-        pltpu.make_async_copy(view(held[i], h), view(outs[i], h), out_sem.at[n]) for n, (i, h) in enumerate(parts)
+        pltpu.make_async_copy(view(i, held[i], h, r), view(i, outs[i], h, r), out_sem.at[n])
+        for n, (i, h, r) in enumerate(parts)
     ]
     for load in loads:
         load.start()
@@ -412,7 +423,7 @@
         out_shape=(jax.ShapeDtypeStruct(queries.shape, BF), weights, weights, weights),
         in_specs=[any_spec] * 4,
         out_specs=[any_spec] * 4,
-        scratch_shapes=[vm(queries.shape, BF)] + [vm(w_first.shape, F32)] * 3 + [dma((7,)), dma((7,))],
+        scratch_shapes=[vm(queries.shape, BF)] + [vm(w_first.shape, F32)] * 3 + [dma((13,)), dma((13,))],
         compiler_params=pltpu.CompilerParams(vmem_limit_bytes=VMEM_BYTES),
         name="hand_out",
     )(*results)

time: 101 us -> 90.6 us (0.90)
  Pallas kernels: 99.9 us -> 89.7 us
    pallas_call x1, Pallas kernels: 93.8 us -> 83.7 us  [on_device(): pl.pallas_call(kernel, out_shape=(jax.ShapeDtypeStruct(queries.shape, BF)...]
where the time goes in v3:
time: 90.6 us; the launch traced here: 90.5 us
  Pallas kernels  89.7 us (99%)
    pallas_call x1, Pallas kernels, on_device(): pl.pallas_call(kernel, out_shape=(jax.ShapeDtypeStruct(queries.shape, BF)...  83.7 us
    pallas_call x1, Pallas kernels, on_device(): pl.pallas_call(hand_out, out_shape=(jax.ShapeDtypeStruct(queries.shape, B...  5.96 us

profile of v3, /device:TPU:1, one launch (start us, length us, event | category | flops | bytes accessed | tf_op | source)
XLA Modules:
  0.0 90.5 jit_solution(10686509352029880874)
XLA Ops:
  0.6 83.7 %layer.1 = (bf16[64,8192]{1,0:T(8,128)(2,1)}, f32[2,512,512]{2,1,0:T(8,128)}, f32[2,512,512]{2,1,0:T(8,128)}, f32[2,512,512]{2,1,0:T(8,128)}) custom-call(bf16[64,8192]{1,0:T(8,128)(2,1)} %q_hbm.1, bf16[64,8192]{1,0:T(8,128)(2,1)} %k_hbm.1, bf16[64,8192]{1,0:T(8,128)(2,1)} %v_hbm.1, bf16[16,64]{1,0:T(8,128)(2,1)} %bitcast.1, f32[2,512,512]{2,1,0:T(8,128)} %w1_hbm.1, ...), custom_call_target="tpu_custom_call" | custom-call | tf_op jit(solution)/shard_map/layer/pallas_call | solution.py:371
  84.4 6.0 %hand_out.1 = (bf16[64,8192]{1,0:T(8,128)(2,1)}, f32[2,512,512]{2,1,0:T(8,128)}, f32[2,512,512]{2,1,0:T(8,128)}, f32[2,512,512]{2,1,0:T(8,128)}) custom-call(bf16[64,8192]{1,0:T(8,128)(2,1)} %get-tuple-element.8.refs_0_, f32[2,512,512]{2,1,0:T(8,128)} %get-tuple-element.9.refs_1_, f32[2,512,512]{2,1,0:T(8,128)} %get-tuple-element.10.refs_2_, ...), custom_call_target="tpu_custom_call" | custom-call | tf_op jit(solution)/shard_map/hand_out/pallas_call | solution.py:421

commit v4 on v3

--- a/solution.py
+++ b/solution.py
@@ -20,7 +20,7 @@
 TILE = 256
 NT = (((1,), (1,)), ((), ()))
 TN = (((0,), (0,)), ((), ()))
-OFFSETS = ((2, 1), (2, 0), (1, 1), (3, 1), (1, 0), (3, 0), (0, 1))
+OFFSETS = ((1, 0), (3, 0), (0, 1), (2, 0), (1, 1), (3, 1), (2, 1))
 BACK = tuple(OFFSETS.index(((4 - dx) % 4, dz)) for dx, dz in OFFSETS)
 OWN = len(OFFSETS)
 
@@ -317,13 +317,13 @@
         lambda: pass_on(0),
         lambda: relay_gather(0),
         lambda: gather(1),
+        lambda: share(0),
         lambda: pass_on(1),
-        lambda: share(0),
+        lambda: newton_own(0),
         lambda: relay_gather(1),
-        lambda: newton_own(0),
+        lambda: newton_second(0),
         lambda: share(1),
         lambda: scatter(q_hbm, qin.at[1], 4 + 1, 1),
-        lambda: newton_second(0),
         lambda: renew_both(0),
         lambda: apply(0),
         lambda: newton_own(1),

time: 90.6 us -> 93.4 us (1.031)
  Pallas kernels: 89.7 us -> 92.5 us
    pallas_call x1, Pallas kernels: 83.7 us -> 86.6 us  [on_device(): pl.pallas_call(kernel, out_shape=(jax.ShapeDtypeStruct(queries.shape, BF)...]
where the time goes in v4:
time: 93.4 us; the launch traced here: 93.3 us
  Pallas kernels  92.5 us (99%)
    pallas_call x1, Pallas kernels, on_device(): pl.pallas_call(kernel, out_shape=(jax.ShapeDtypeStruct(queries.shape, BF)...  86.6 us
    pallas_call x1, Pallas kernels, on_device(): pl.pallas_call(hand_out, out_shape=(jax.ShapeDtypeStruct(queries.shape, B...  5.96 us

profile of v4, /device:TPU:1, one launch (start us, length us, event | category | flops | bytes accessed | tf_op | source)
XLA Modules:
  0.0 93.3 jit_solution(13370870898314872827)
XLA Ops:
  0.6 86.6 %layer.1 = (bf16[64,8192]{1,0:T(8,128)(2,1)}, f32[2,512,512]{2,1,0:T(8,128)}, f32[2,512,512]{2,1,0:T(8,128)}, f32[2,512,512]{2,1,0:T(8,128)}) custom-call(bf16[64,8192]{1,0:T(8,128)(2,1)} %q_hbm.1, bf16[64,8192]{1,0:T(8,128)(2,1)} %k_hbm.1, bf16[64,8192]{1,0:T(8,128)(2,1)} %v_hbm.1, bf16[16,64]{1,0:T(8,128)(2,1)} %bitcast.1, f32[2,512,512]{2,1,0:T(8,128)} %w1_hbm.1, ...), custom_call_target="tpu_custom_call" | custom-call | tf_op jit(solution)/shard_map/layer/pallas_call | solution.py:371
  87.2 6.0 %hand_out.1 = (bf16[64,8192]{1,0:T(8,128)(2,1)}, f32[2,512,512]{2,1,0:T(8,128)}, f32[2,512,512]{2,1,0:T(8,128)}, f32[2,512,512]{2,1,0:T(8,128)}) custom-call(bf16[64,8192]{1,0:T(8,128)(2,1)} %get-tuple-element.8.refs_0_, f32[2,512,512]{2,1,0:T(8,128)} %get-tuple-element.9.refs_1_, f32[2,512,512]{2,1,0:T(8,128)} %get-tuple-element.10.refs_2_, ...), custom_call_target="tpu_custom_call" | custom-call | tf_op jit(solution)/shard_map/hand_out/pallas_call | solution.py:421

commit v5 on v3

--- a/solution.py
+++ b/solution.py
@@ -80,7 +80,7 @@
         return pl.ds(pl.multiple_of((2 * p + h) * DH, DH), DH)
 
     def scatter(src, land, i, h):
-        for p, b in zip(peers, BACK):
+        for p, b in reversed(tuple(zip(peers, BACK))):
             remote(src.at[:, columns(p, h)], land.at[slot(b)], a2a_s.at[i], a2a_r.at[i], head=p).start()
         pltpu.make_async_copy(src.at[:, columns(hi, h)], land.at[slot(OWN)], a2a_r.at[i]).start()
         track("a2a", i, land.at[pl.ds(0, SPAN - ROWS)], land, a2a_s, a2a_r)

time: 90.6 us -> 90.6 us (level)
  no operation moved by 1% of the time
where the time goes in v5:
time: 90.6 us; the launch traced here: 90.5 us
  Pallas kernels  89.7 us (99%)
    pallas_call x1, Pallas kernels, on_device(): pl.pallas_call(kernel, out_shape=(jax.ShapeDtypeStruct(queries.shape, BF)...  83.8 us
    pallas_call x1, Pallas kernels, on_device(): pl.pallas_call(hand_out, out_shape=(jax.ShapeDtypeStruct(queries.shape, B...  5.96 us

profile of v5, /device:TPU:1, one launch (start us, length us, event | category | flops | bytes accessed | tf_op | source)
XLA Modules:
  0.0 90.5 jit_solution(6471821351961994762)
XLA Ops:
  0.6 83.8 %layer.1 = (bf16[64,8192]{1,0:T(8,128)(2,1)}, f32[2,512,512]{2,1,0:T(8,128)}, f32[2,512,512]{2,1,0:T(8,128)}, f32[2,512,512]{2,1,0:T(8,128)}) custom-call(bf16[64,8192]{1,0:T(8,128)(2,1)} %q_hbm.1, bf16[64,8192]{1,0:T(8,128)(2,1)} %k_hbm.1, bf16[64,8192]{1,0:T(8,128)(2,1)} %v_hbm.1, bf16[16,64]{1,0:T(8,128)(2,1)} %bitcast.1, f32[2,512,512]{2,1,0:T(8,128)} %w1_hbm.1, ...), custom_call_target="tpu_custom_call" | custom-call | tf_op jit(solution)/shard_map/layer/pallas_call | solution.py:371
  84.4 6.0 %hand_out.1 = (bf16[64,8192]{1,0:T(8,128)(2,1)}, f32[2,512,512]{2,1,0:T(8,128)}, f32[2,512,512]{2,1,0:T(8,128)}, f32[2,512,512]{2,1,0:T(8,128)}) custom-call(bf16[64,8192]{1,0:T(8,128)(2,1)} %get-tuple-element.8.refs_0_, f32[2,512,512]{2,1,0:T(8,128)} %get-tuple-element.9.refs_1_, f32[2,512,512]{2,1,0:T(8,128)} %get-tuple-element.10.refs_2_, ...), custom_call_target="tpu_custom_call" | custom-call | tf_op jit(solution)/shard_map/hand_out/pallas_call | solution.py:421
